TPU v7x, 32 devices: a whole 2x2x4 slice. The times are simulated.
32 devices in a mesh: dp: 8 (over z, y), space: 4 (over x, core).
Axes of the slice: x: 2, y: 2, z: 4, core: 2. Of those that a mesh axis runs over, the one named last changes fastest.
Arguments:
- activations: bfloat16 [8, 64, 32, 48, 128], P('dp', None, 'space'), may hold values from -6 to 6
- cotangent: bfloat16 [8, 64, 32, 48, 128], P('dp', None, 'space'), may hold values from -6 to 6
- mode_weights: bfloat16 [2048, 64, 128], P(('space', 'dp')), may hold values from -6 to 6
- pointwise: bfloat16 [64, 64], replicated, may hold values from -0.75 to 0.75
- offsets: float32 [64], replicated, may hold values from -3 to 3
Outputs:
- grad_in: bfloat16 [8, 64, 32, 48, 128], P('dp', None, 'space')
- grad_spectral: float32 [2048, 64, 128], P(('space', 'dp'))
All inputs are finite; a program needn't handle non-finite values.
Results may differ from a plain program's by a relative error of at most 0.02.
Values may be sent and summed in bfloat16 or wider, within the bound.
No kernel may reach another device: no remote copies, remote signals or barrier semaphores. Data moves between devices by JAX's collectives and lax.ppermute only.
A program may use at most 128 MiB of HBM per device.

v0:
```python
import functools
import math

import jax
import jax.numpy as jnp
import ml_dtypes
import numpy as np
from jax import lax
from jax.experimental import pallas as pl
from jax.experimental.pallas import tpu as pltpu
from jax.sharding import PartitionSpec as P

MX = 16
MY = 16
MZ = 8
NX = 32


def centered(count):
    index = jnp.arange(count, dtype=jnp.int32)
    return jnp.where(index < count // 2, index, index - count)


def plane_tables(rows_y, rows_z, modes_y, modes_z):
    along_y = jnp.arange(rows_y, dtype=jnp.int32)[:, None, None, None]
    along_z = jnp.arange(rows_z, dtype=jnp.int32)[None, :, None, None]
    freq_y = centered(modes_y)[None, None, :, None]
    freq_z = jnp.arange(modes_z, dtype=jnp.int32)[None, None, None, :]
    phase = jnp.mod(freq_y * along_y * rows_z + freq_z * along_z * rows_y, rows_y * rows_z)
    theta = phase.astype(jnp.float32) * (2.0 * math.pi / (rows_y * rows_z))
    cosine = jnp.cos(theta)
    sine = jnp.sin(theta)
    forward = jnp.stack([cosine, -sine], -1).reshape(rows_y * rows_z, modes_y * modes_z * 2)
    scaled = jnp.where(freq_z == 0, 1.0, 2.0).astype(jnp.float32) / (rows_y * rows_z)
    inverse = (
        jnp.stack([cosine * scaled, -sine * scaled], -1)
        .reshape(rows_y * rows_z, modes_y * modes_z * 2)
        .T
    )
    return (forward.astype(jnp.bfloat16), inverse.astype(jnp.bfloat16))


def line_tables(length, modes):
    along = jnp.arange(length, dtype=jnp.int32)[:, None]
    freq = centered(modes)[None, :]
    phase = jnp.mod(freq * along, length)
    theta = phase.astype(jnp.float32) * (2.0 * math.pi / length)
    cosine = jnp.cos(theta)
    sine = jnp.sin(theta)
    first = jnp.stack([cosine, -sine], -1)
    second = jnp.stack([sine, cosine], -1)
    forward = jnp.stack([first, second], 1).reshape(2 * length, 2 * modes)
    inv_first = jnp.stack([cosine.T, sine.T], -1) / length
    inv_second = jnp.stack([-sine.T, cosine.T], -1) / length
    inverse = jnp.stack([inv_first, inv_second], 1).reshape(2 * modes, 2 * length)
    return (forward.astype(jnp.bfloat16), inverse.astype(jnp.bfloat16))


def expand_weights(weights):
    half = weights.shape[1]
    real_part = weights[:, :, :half]
    imag_part = weights[:, :, half:]
    upper = jnp.concatenate([real_part, imag_part], axis=2)
    lower = jnp.concatenate([-imag_part, real_part], axis=2)
    return jnp.concatenate([upper, lower], axis=1)


def outer_sum(left, right):
    return jnp.einsum("mbi,mbo->mio", left, right, preferred_element_type=jnp.float32)


def weight_terms(spec_in, spec_grad):
    half = spec_in.shape[2] // 2
    in_real = spec_in[:, :, :half]
    in_imag = spec_in[:, :, half:]
    gr_real = spec_grad[:, :, :half]
    gr_imag = spec_grad[:, :, half:]
    real_term = outer_sum(in_real, gr_real) + outer_sum(in_imag, gr_imag)
    imag_term = outer_sum(in_real, gr_imag) - outer_sum(in_imag, gr_real)
    return jnp.concatenate([real_term, imag_term], axis=2)


def to_modes(slab, table, modes_x):
    samples, channels, width, pairs = slab.shape
    moved = lax.all_to_all(slab, "space", split_axis=3, concat_axis=2, tiled=True)
    length = moved.shape[2]
    local = moved.shape[3] // 2
    lines = moved.reshape(samples, channels, length, local, 2).transpose(0, 1, 3, 2, 4)
    lines = lines.reshape(samples, channels, local, 2 * length)
    spectra = jnp.dot(lines, table, preferred_element_type=jnp.float32).astype(jnp.bfloat16)
    spectra = spectra.reshape(samples, channels, local, modes_x, 2).transpose(2, 3, 0, 4, 1)
    return spectra.reshape(local * modes_x, samples, 2 * channels)


def to_slab(spectra, table, modes_x, channels):
    count, samples, doubled = spectra.shape
    local = count // modes_x
    lines = spectra.reshape(local, modes_x, samples, 2, channels).transpose(2, 4, 0, 1, 3)
    lines = lines.reshape(samples, channels, local, 2 * modes_x)
    lines = jnp.dot(lines, table, preferred_element_type=jnp.float32).astype(jnp.bfloat16)
    length = lines.shape[3] // 2
    lines = lines.reshape(samples, channels, local, length, 2).transpose(0, 1, 3, 2, 4)
    lines = lines.reshape(samples, channels, length, 2 * local)
    return lax.all_to_all(lines, "space", split_axis=2, concat_axis=3, tiled=True)


def to_owners(spectra):
    return lax.all_to_all(spectra, "dp", split_axis=0, concat_axis=1, tiled=True)


def from_owners(spectra):
    return lax.all_to_all(spectra, "dp", split_axis=1, concat_axis=0, tiled=True)


def gelu_slope(value):
    cdf = 0.5 * (1.0 + lax.erf(value * 0.7071067811865476))
    density = jnp.exp(-0.5 * value * value) * 0.3989422804014327
    return cdf + value * density


def general_body(activations, cotangent, mode_weights, pointwise, offsets):
    samples, channels, width, rows_y, rows_z = activations.shape
    plane_fwd, plane_inv = plane_tables(rows_y, rows_z, MY, MZ)
    line_fwd, line_inv = line_tables(NX, MX)
    flat = activations.reshape(samples, channels, width, rows_y * rows_z)
    planes = jnp.dot(flat, plane_fwd, preferred_element_type=jnp.float32).astype(jnp.bfloat16)
    spec_in = to_modes(planes, line_fwd, MX)
    blocks = expand_weights(mode_weights)
    held_in = to_owners(spec_in)
    held_out = jnp.einsum(
        "mbi,mio->mbo", held_in, blocks, preferred_element_type=jnp.float32
    ).astype(jnp.bfloat16)
    spec_out = from_owners(held_out)
    returned = to_slab(spec_out, line_inv, MX, channels)
    spectral = jnp.dot(returned, plane_inv, preferred_element_type=jnp.float32)
    local_part = jnp.einsum("io,bixn->boxn", pointwise, flat, preferred_element_type=jnp.float32)
    summed = spectral + local_part + offsets[None, :, None, None]
    upstream = cotangent.reshape(flat.shape).astype(jnp.float32)
    slope_grad = (upstream * gelu_slope(summed)).astype(jnp.bfloat16)
    back_plane = jnp.dot(slope_grad, plane_inv.T, preferred_element_type=jnp.float32).astype(
        jnp.bfloat16
    )
    spec_grad = to_modes(back_plane, line_inv.T, MX)
    held_grad = to_owners(spec_grad)
    held_dx = jnp.einsum(
        "mbo,mio->mbi", held_grad, blocks, preferred_element_type=jnp.float32
    ).astype(jnp.bfloat16)
    spec_dx = from_owners(held_dx)
    grad_spectral = weight_terms(held_in, held_grad)
    line_dx = to_slab(spec_dx, line_fwd.T, MX, channels)
    total = jnp.dot(line_dx, plane_fwd.T, preferred_element_type=jnp.float32)
    total = total + jnp.einsum(
        "io,boxn->bixn", pointwise, slope_grad, preferred_element_type=jnp.float32
    )
    grad_in = total.astype(jnp.bfloat16).reshape(activations.shape)
    return (grad_in, grad_spectral)


BF16 = jnp.bfloat16
F32 = jnp.float32
GROUP = 16
TILE = 8
SLOTS = 4
STEPS = GROUP // SLOTS
MIB = 1024 * 1024


def rounded(table):
    return np.asarray(table, np.float32).astype(ml_dtypes.bfloat16)


def angles(freq, points, length):
    phase = np.mod(np.outer(freq, points), length)
    return (phase * (2.0 * math.pi / length)).astype(np.float64)


def signed(count):
    index = np.arange(count)
    return np.where(index < count // 2, index, index - count)


def z_base(rows_z):
    theta = angles(np.arange(MZ), np.arange(rows_z), rows_z)
    pair = np.stack([np.cos(theta), -np.sin(theta)])
    table = np.repeat(pair.reshape(2 * MZ, rows_z), GROUP, axis=0).T
    return rounded(table).astype(np.float32)


def y_table(rows_y, width):
    theta = angles(signed(MY), np.arange(rows_y), rows_y)
    cosine, sine = np.cos(theta), np.sin(theta)
    turn = np.stack([np.stack([cosine, sine]), np.stack([-sine, cosine])])
    table = np.einsum("rsjy,xw->jxrswy", turn, np.eye(width))
    return rounded(table.reshape(MY * width * 2, 2 * width * rows_y))


def x_tables(samples, slabs, length):
    theta = angles(signed(MX), np.arange(length), length)
    cosine, sine = np.cos(theta), np.sin(theta)
    forward = np.stack([np.stack([cosine, sine]), np.stack([-sine, cosine])])
    inverse = np.stack([np.stack([cosine, sine]), np.stack([-sine, cosine])]) / length
    same = np.eye(samples)
    rows = MX * 2 * samples

    def lay(turn):
        turn = turn.reshape(2, 2, MX, slabs, length // slabs)
        table = np.einsum("arqsx,bd->qabsdxr", turn, same)
        return rounded(table.reshape(rows, samples * length * 2))

    return lay(forward), lay(inverse)


def dot(left, right):
    return jnp.dot(left, right, preferred_element_type=F32)


def gelu_slope_rows(value):
    decay = jnp.exp2(value * value * (-0.5 * math.log2(math.e))).astype(BF16)
    cdf = (0.5 + 0.5 * lax.erf(value * math.sqrt(0.5))).astype(BF16)
    density = value.astype(BF16) * jnp.asarray(1.0 / math.sqrt(2.0 * math.pi), BF16)
    return cdf + density * decay


def over(index, size):
    return lax.shift_right_logical(index, jnp.int32(size.bit_length() - 1))


def within(index, size):
    return jnp.bitwise_and(index, jnp.int32(size - 1))


def fill_z(base, table):
    rows_z, lanes = base.shape
    owner = within(lax.broadcasted_iota(jnp.int32, (rows_z, lanes), 1), GROUP)
    values = base[...]
    for c in range(GROUP):
        table[c * rows_z : (c + 1) * rows_z] = jnp.where(owner == c, values, 0.0).astype(BF16)


def fill_z_back(base, table):
    lanes, rows_z = base.shape
    owner = within(lax.broadcasted_iota(jnp.int32, (lanes, rows_z), 0), GROUP)
    values = base[...]
    for c in range(GROUP):
        first = c % SLOTS * rows_z
        table[c // SLOTS, :, first : first + rows_z] = jnp.where(owner == c, values, 0.0).astype(BF16)


def grouped(lane, per, channels):
    c = within(lane, channels)
    return over(c, GROUP) * (MZ * GROUP) + over(lane, channels) * GROUP + within(c, GROUP)


def fill_order(per, channels, back, table):
    count = table.shape[0]
    row = lax.broadcasted_iota(jnp.int32, (count, count), 0)
    column = lax.broadcasted_iota(jnp.int32, (count, count), 1)
    if back:
        same = grouped(row[:, :1], per, channels) == column
    else:
        same = row == grouped(column[:1], per, channels)
    table[...] = jnp.where(same, 1.0, 0.0).astype(BF16)


def deliver(spectra, ytab, order, scale, message, per, channels):
    groups = channels // GROUP
    rows = spectra.shape[0] // groups
    wide = spectra.shape[1] // 2
    halves = []
    for r in range(2):
        blocks = [spectra[g * rows : (g + 1) * rows, r * wide : (r + 1) * wide] for g in range(groups)]
        halves.append(jnp.concatenate(blocks, axis=1).astype(BF16))
    planes = dot(ytab[...], jnp.concatenate(halves, axis=0))
    if scale is not None:
        planes = planes * scale[...]
    ordered = dot(planes.astype(BF16), order[...]).astype(BF16)
    parts = MZ // per
    count = message.shape[1]
    lanes = per * channels
    for part in range(parts):
        block = ordered[:, part * lanes : (part + 1) * lanes]
        for j in range(MY):
            message[j * parts + part] = block[j * count : (j + 1) * count]


def receive(message, order_back, ytab_back, scale, held, per):
    parts = MZ // per
    blocks = message[...]
    blocks = blocks.reshape(MY, parts, *blocks.shape[1:])
    lanes = [blocks[:, part].reshape(-1, blocks.shape[3]) for part in range(parts)]
    ordered = dot(jnp.concatenate(lanes, axis=1), order_back[...]).astype(BF16)
    lines = dot(ytab_back[...], ordered)
    if scale is not None:
        lines = lines * scale[...]
    lines = lines.astype(BF16)
    rows = lines.shape[0] // 2
    wide = MZ * GROUP
    for group in range(held.shape[0] // rows):
        piece = lines[:, group * wide : (group + 1) * wide]
        held[group * rows : (group + 1) * rows] = jnp.concatenate([piece[:rows], piece[rows:]], axis=1)


class Move:
    def __init__(self, source, target, sems):
        self.source, self.target, self.sems = source, target, sems
        self.groups = target.shape[0] // GROUP

    def copies(self, step):
        for g in range(self.groups):
            run = pl.ds(g * GROUP + step * SLOTS, SLOTS)
            sem = self.sems.at[step * self.groups + g]
            yield pltpu.make_async_copy(self.source.at[run], self.target.at[run], sem)

    def start(self, step):
        for copy in self.copies(step):
            copy.start()

    def wait(self, step):
        for copy in self.copies(step):
            copy.wait()


def start_all(moves, step):
    for each in moves:
        each.start(step)


def add_spectra(field, ztab, first, count, spectra):
    groups = field.shape[0] // GROUP
    rows_z = field.shape[-1]
    rows = spectra.shape[0] // groups
    table = ztab[pl.ds(pl.multiple_of(first * rows_z, count * rows_z), count * rows_z)]
    lanes = [
        jnp.concatenate([field[g * GROUP + first + slot].reshape(rows, rows_z) for g in range(groups)], axis=0)
        for slot in range(count)
    ]
    spectra[...] += dot(jnp.concatenate(lanes, axis=1), table)


def plane_kernel(
    per, channels, field, base_far, ytab_far, message, ztab, order, spectra, buffer, base, ytab, sems, table_sems
):
    incoming = Move(field.at[0], buffer, sems)
    base_copy = pltpu.make_async_copy(base_far, base, table_sems.at[0])
    ytab_copy = pltpu.make_async_copy(ytab_far, ytab, table_sems.at[1])
    base_copy.start()
    incoming.start(0)
    fill_order(per, channels, False, order)
    spectra[...] = jnp.zeros_like(spectra)
    incoming.start(1)
    base_copy.wait()
    fill_z(base, ztab)
    incoming.start(2)
    ytab_copy.start()
    incoming.start(3)

    @pl.loop(0, STEPS)
    def _(step):
        incoming.wait(step)
        add_spectra(buffer, ztab, step * SLOTS, SLOTS, spectra)

    ytab_copy.wait()
    deliver(spectra, ytab, order, None, message, per, channels)


def slope_kernel(
    per, channels, arrived, local, cotangent, base, base_back, ytab, ytab_back, scale,
    slope, message, ztab, ztab_back, order, held, spectra, local_in, cotangent_in, result, first_sum, second_sum,
    local_sems, cotangent_sems, result_sems,
):
    width, rows_y, rows_z = local.shape[1:]
    groups = channels // GROUP
    rows = width * rows_y
    wide = 2 * rows_y
    incoming = (Move(local, local_in, local_sems), Move(cotangent.at[0], cotangent_in, cotangent_sems))
    outgoing = Move(result, slope, result_sems)
    start_all(incoming, 0)
    fill_order(per, channels, True, order)
    receive(arrived, order, ytab_back, scale, held, per)
    start_all(incoming, 1)
    fill_z_back(base_back, ztab_back)
    fill_z(base, ztab)
    start_all(incoming, 2)
    fill_order(per, channels, False, order)
    spectra[...] = jnp.zeros_like(spectra)
    start_all(incoming, 3)

    @pl.loop(0, STEPS)
    def _(step):
        for each in incoming:
            each.wait(step)
        for pair, total in enumerate((first_sum, second_sum)):
            total[...] = dot(held[...], ztab_back[step, :, 2 * pair * rows_z : 2 * (pair + 1) * rows_z])
        for pair, total in enumerate((first_sum, second_sum)):
            for g in range(groups):
                for offset in range(2):
                    c = g * GROUP + step * SLOTS + 2 * pair + offset
                    for x in range(0, width, 2):
                        place = g * rows + x * rows_y
                        value = total[place : place + wide, offset * rows_z : (offset + 1) * rows_z]
                        value = value + local_in[c, x : x + 2].reshape(wide, rows_z).astype(F32)
                        upstream = cotangent_in[c, x : x + 2].reshape(wide, rows_z)
                        answer = upstream * gelu_slope_rows(value)
                        result[c, x : x + 2] = answer.reshape(2, rows_y, rows_z)
            add_spectra(result, ztab, step * SLOTS + 2 * pair, 2, spectra)
        outgoing.start(step)

    deliver(spectra, ytab, order, scale, message, per, channels)
    for step in range(STEPS):
        outgoing.wait(step)


def field_kernel(
    per, channels, arrived, local, base_back, ytab_back, out, ztab_back, order, held, local_in, result,
    local_sems, result_sems,
):
    width, rows_y, rows_z = local.shape[1:]
    groups = channels // GROUP
    rows = width * rows_y
    incoming = Move(local, local_in, local_sems)
    outgoing = Move(result, out.at[0], result_sems)
    incoming.start(0)
    fill_order(per, channels, True, order)
    incoming.start(1)
    receive(arrived, order, ytab_back, None, held, per)
    incoming.start(2)
    fill_z_back(base_back, ztab_back)
    incoming.start(3)

    @pl.loop(0, STEPS)
    def _(step):
        incoming.wait(step)
        for pair in range(SLOTS // 2):
            total = dot(held[...], ztab_back[step, :, 2 * pair * rows_z : 2 * (pair + 1) * rows_z])
            for g in range(groups):
                for offset in range(2):
                    c = g * GROUP + step * SLOTS + 2 * pair + offset
                    value = total[g * rows : (g + 1) * rows, offset * rows_z : (offset + 1) * rows_z]
                    value = value + local_in[c].reshape(rows, rows_z).astype(F32)
                    result[c] = value.astype(BF16).reshape(width, rows_y, rows_z)
        outgoing.start(step)

    for step in range(STEPS):
        outgoing.wait(step)


def pointwise_kernel(turned, field, mix, offsets, out, table, shift):
    channels = mix.shape[0]
    width, rows_y, rows_z = field.shape[1:]
    size = channels * TILE

    @pl.when(pl.program_id(0) == 0)
    def _():
        row = over(lax.broadcasted_iota(jnp.int32, (size, channels), 0), TILE)
        column = lax.broadcasted_iota(jnp.int32, (size, channels), 1)
        spread = jnp.where(row == column, 1.0, 0.0).astype(BF16)
        tall = lax.dot_general(
            spread, mix[...], (((1,), (1 if turned else 0,)), ((), ())), preferred_element_type=F32
        ).astype(BF16)
        whole = lax.dot_general(
            tall, spread, (((1,), (1,)), ((), ())), preferred_element_type=F32
        )
        place = within(lax.broadcasted_iota(jnp.int32, (size, size), 0), TILE)
        other = within(lax.broadcasted_iota(jnp.int32, (size, size), 1), TILE)
        table[...] = jnp.where(place == other, whole, 0.0).astype(BF16)
        if offsets is not None:
            for c in range(channels):
                shift[c] = jnp.full((1, rows_z), offsets[c], F32)

    for start in range(0, rows_y, 2 * TILE):
        pieces = [field[:, x, start : start + 2 * TILE, :].astype(F32) for x in range(width)]
        halves = []
        for row in range(0, 2 * TILE, TILE):
            rows = [piece[:, row : row + TILE].reshape(size, rows_z).astype(BF16) for piece in pieces]
            halves.append(dot(table[...], jnp.concatenate(rows, axis=1)))
        for x in range(width):
            values = [
                half[:, x * rows_z : (x + 1) * rows_z].reshape(channels, TILE, rows_z) for half in halves
            ]
            value = jnp.concatenate(values, axis=1)
            if offsets is not None:
                value = value + shift[...]
            out[:, x, start : start + 2 * TILE, :] = value.astype(BF16)


def spread_pair(first, second):
    nothing = jnp.zeros_like(first)
    upper = jnp.concatenate([first, nothing], axis=1)
    lower = jnp.concatenate([nothing, second], axis=1)
    return jnp.concatenate([upper, lower], axis=0)


def low_half(shape):
    return lax.broadcasted_iota(jnp.int32, shape, 1) < shape[1] // 2


def mix_kernel(per, samples, arrived, weights, line, line_back, spec_in, message, held):
    rows = 2 * samples
    lanes = 2 * weights.shape[1]
    low = low_half((samples, lanes))
    flat = arrived[...].reshape(-1, arrived.shape[2])
    spectra = dot(line[...], flat).astype(BF16)
    spec_in[...] = spectra
    for q in range(MX):
        for first in range(0, per, 2):
            block = spread_pair(weights[first * MX + q], weights[(first + 1) * MX + q])
            place = first // 2 * lanes
            terms = dot(spectra[q * rows : (q + 1) * rows, place : place + lanes], block)
            mixed = []
            for side in range(2):
                part = terms[:, side * lanes : (side + 1) * lanes]
                turned = pltpu.roll(part[samples:], lanes // 2, 1)
                mixed.append(part[:samples] + jnp.where(low, -turned, turned))
            real = jnp.where(low, mixed[0], pltpu.roll(mixed[1], lanes // 2, 1))
            imag = jnp.where(low, pltpu.roll(mixed[0], lanes // 2, 1), mixed[1])
            held[q * rows : (q + 1) * rows, place : place + lanes] = jnp.concatenate(
                [real, imag], axis=0
            ).astype(BF16)
    message[...] = dot(line_back[...], held[...]).astype(BF16).reshape(message.shape)


def mix_back_kernel(per, samples, arrived, weights, line, line_back, pairs, message, held):
    rows = 2 * samples
    lanes = 2 * weights.shape[1]
    low = low_half((samples, lanes))
    flat = arrived[...].reshape(-1, arrived.shape[2])
    spectra = dot(line[...], flat).astype(BF16).astype(F32)
    for q in range(MX):
        for first in range(0, per, 2):
            block = spread_pair(weights[first * MX + q], weights[(first + 1) * MX + q])
            place = first // 2 * lanes
            real = spectra[q * rows : q * rows + samples, place : place + lanes]
            imag = spectra[q * rows + samples : (q + 1) * rows, place : place + lanes]
            real_turned = pltpu.roll(real, lanes // 2, 1)
            imag_turned = pltpu.roll(imag, lanes // 2, 1)
            left = [jnp.where(low, real, imag_turned), jnp.where(low, imag, -real_turned)]
            right = [jnp.where(low, real_turned, imag), jnp.where(low, imag_turned, -real)]
            pair = jnp.concatenate(
                [jnp.concatenate(left, axis=0), jnp.concatenate(right, axis=0)], axis=1
            ).astype(BF16)
            pairs[q * rows : (q + 1) * rows, 2 * place : 2 * (place + lanes)] = pair
            held[q * rows : (q + 1) * rows, place : place + lanes] = lax.dot_general(
                pair, block, (((1,), (1,)), ((), ())), preferred_element_type=F32
            ).astype(BF16)
    message[...] = dot(line_back[...], held[...]).astype(BF16).reshape(message.shape)


def weight_kernel(per, samples, spec_in, pairs, out):
    rows = 2 * samples
    lanes = out.shape[2]
    half = lanes // 2
    for q in range(MX):
        for first in range(0, per, 2):
            place = first // 2 * lanes
            left = spec_in[q * rows : (q + 1) * rows, place : place + lanes]
            right = pairs[q * rows : (q + 1) * rows, 2 * place : 2 * (place + lanes)]
            outer = lax.dot_general(
                left, right, (((0,), (0,)), ((), ())), preferred_element_type=F32
            )
            out[first * MX + q] = outer[:half, :lanes]
            out[(first + 1) * MX + q] = outer[half:, lanes:]


def whole(array):
    return pl.BlockSpec(array.shape, lambda *step: (0,) * len(array.shape))


def shaped(shape, dtype):
    return jax.ShapeDtypeStruct(shape, dtype)


def params(mib):
    return pltpu.CompilerParams(vmem_limit_bytes=mib * MIB)


def cost(flops, moved, steep=0):
    return pl.CostEstimate(flops=flops, bytes_accessed=moved, transcendentals=steep)


def body(mesh_axes, devices, slabs, activations, cotangent, mode_weights, pointwise, offsets):
    _, channels, width, rows_y, rows_z = activations.shape
    samples = devices // slabs
    per = MY * MZ // devices
    groups = channels // GROUP
    field = activations.shape[1:]
    count = math.prod(field)
    base = z_base(rows_z)
    ytab = y_table(rows_y, width)
    line_fwd, line_inv = x_tables(samples, slabs, NX)
    weight = np.where(np.arange(MZ) == 0, 1.0, 2.0) / (rows_y * rows_z)
    scale = np.tile(np.repeat(weight, GROUP), groups).astype(np.float32)[None]
    base_t, ytab_t = (np.ascontiguousarray(t.T) for t in (base, ytab))
    fwd_t, inv_t = (np.ascontiguousarray(t.T) for t in (line_fwd, line_inv))
    message = shaped((devices, 2 * width, per * channels), BF16)
    spectra = shaped((MX * 2 * samples, per * channels), BF16)
    ztab = pltpu.VMEM((GROUP * rows_z, 2 * MZ * GROUP), BF16)
    ztab_t = pltpu.VMEM((STEPS, 2 * MZ * GROUP, SLOTS * rows_z), BF16)
    order = pltpu.VMEM((MZ * channels, MZ * channels), BF16)
    rows = groups * width * rows_y
    held = pltpu.VMEM((rows, 2 * MZ * GROUP), BF16)
    sums = pltpu.VMEM((rows, 2 * MZ * GROUP), F32)
    pair_sums = pltpu.VMEM((rows, 2 * rows_z), F32)
    buffer = pltpu.VMEM(field, BF16)
    sems = pltpu.SemaphoreType.DMA((STEPS * groups,))
    far = pl.BlockSpec(memory_space=pltpu.HBM)
    far_field = pltpu.HBM(field, BF16)

    def kept_far(array):
        return pltpu.with_memory_space_constraint(array, pltpu.HBM)

    plane_flops = 2 * count * 2 * MZ * GROUP

    def exchange(array):
        return lax.all_to_all(array, mesh_axes, split_axis=0, concat_axis=0, tiled=True)

    def mix_points(values, turned, shifts):
        step = 2
        block = pl.BlockSpec((channels, step, rows_y, rows_z), lambda x: (0, x, 0, 0))
        kernel = functools.partial(pointwise_kernel, turned)
        specs = [block, whole(pointwise)]
        operands = [values, pointwise]
        if shifts is None:
            run = lambda a, b, *rest: kernel(a, b, None, *rest)
        else:
            run = kernel
            specs.append(pl.BlockSpec(memory_space=pltpu.SMEM))
            operands.append(shifts)
        return pl.pallas_call(
            run,
            grid=(width // step,),
            in_specs=specs,
            out_specs=block,
            out_shape=far_field,
            scratch_shapes=[
                pltpu.VMEM((channels * TILE, channels * TILE), BF16),
                pltpu.VMEM((channels, 1, rows_z), F32),
            ],
            compiler_params=params(32),
            cost_estimate=cost(2 * count * channels * TILE, 4 * count),
        )(*operands)

    planes = pl.pallas_call(
        functools.partial(plane_kernel, per, channels),
        in_specs=[far, far, far],
        out_specs=whole(message),
        out_shape=message,
        scratch_shapes=[
            ztab,
            order,
            sums,
            buffer,
            pltpu.VMEM(base.shape, F32),
            pltpu.VMEM(ytab.shape, BF16),
            sems,
            pltpu.SemaphoreType.DMA((2,)),
        ],
        compiler_params=params(32),
        cost_estimate=cost(plane_flops, 2 * count),
    )(kept_far(activations), kept_far(base), kept_far(ytab))
    arrived = exchange(planes)
    local = mix_points(kept_far(activations.reshape(field)), True, offsets)
    arrived, local = lax.optimization_barrier((arrived, local))
    spec_in, mixed = pl.pallas_call(
        functools.partial(mix_kernel, per, samples),
        out_shape=(spectra, message),
        scratch_shapes=[pltpu.VMEM(spectra.shape, BF16)],
        compiler_params=params(16),
        cost_estimate=cost(10**8, 2 * mode_weights.size),
    )(arrived, mode_weights, line_fwd, inv_t)
    returned = exchange(mixed)
    slope, back_plane = pl.pallas_call(
        functools.partial(slope_kernel, per, channels),
        in_specs=[whole(message), far, far]
        + [whole(t) for t in (base, base_t, ytab, ytab_t, scale)],
        out_specs=(far, whole(message)),
        out_shape=(far_field, message),
        scratch_shapes=[ztab, ztab_t, order, held, sums]
        + [buffer] * 3
        + [pair_sums] * 2
        + [sems] * 3,
        compiler_params=params(32),
        cost_estimate=cost(2 * plane_flops, 6 * count, 2 * count),
    )(returned, kept_far(local), kept_far(cotangent), base, base_t, ytab, ytab_t, scale)
    arrived_back = exchange(back_plane)
    local_back = mix_points(kept_far(slope), False, None)
    arrived_back, local_back = lax.optimization_barrier((arrived_back, local_back))
    pairs, mixed_back = pl.pallas_call(
        functools.partial(mix_back_kernel, per, samples),
        out_shape=(shaped((spectra.shape[0], 2 * spectra.shape[1]), BF16), message),
        scratch_shapes=[pltpu.VMEM(spectra.shape, BF16)],
        compiler_params=params(16),
        cost_estimate=cost(10**8, 2 * mode_weights.size),
    )(arrived_back, mode_weights, line_inv, fwd_t)
    returned_back = exchange(mixed_back)
    grad_spectral = pl.pallas_call(
        functools.partial(weight_kernel, per, samples),
        out_shape=shaped(mode_weights.shape, F32),
        compiler_params=params(16),
        cost_estimate=cost(10**8, 4 * mode_weights.size),
    )(spec_in, pairs)
    grad_in = pl.pallas_call(
        functools.partial(field_kernel, per, channels),
        in_specs=[whole(message), far, whole(base_t), whole(ytab_t)],
        out_specs=far,
        out_shape=shaped(activations.shape, BF16),
        scratch_shapes=[ztab_t, order, held, buffer, buffer, sems, sems],
        compiler_params=params(32),
        cost_estimate=cost(plane_flops, 4 * count),
    )(returned_back, kept_far(local_back), base_t, ytab_t)
    return (grad_in, grad_spectral)


def chosen_body(mesh_axes, devices, slabs, activations, cotangent, mode_weights, pointwise, offsets):
    samples, channels, width, rows_y, rows_z = activations.shape
    per = MY * MZ // devices
    fits = (
        samples == 1
        and MY * MZ % devices == 0
        and per in (2, 4, 8)
        and width % 8 == 0
        and channels == 64
        and rows_y % TILE == 0
        and rows_z == 128
    )
    plan = functools.partial(body, mesh_axes, devices, slabs) if fits else general_body
    return plan(activations, cotangent, mode_weights, pointwise, offsets)


def solution(mesh):
    slabs = mesh.shape["space"]
    devices = slabs * mesh.shape["dp"]
    return jax.shard_map(
        functools.partial(chosen_body, ("space", "dp"), devices, slabs),
        mesh=mesh,
        in_specs=(
            P("dp", None, "space", None, None),
            P("dp", None, "space", None, None),
            P(("space", "dp"), None, None),
            P(),
            P(),
        ),
        out_specs=(P("dp", None, "space", None, None), P(("space", "dp"), None, None)),
        check_vma=False,
    )
```

profile of v0, /device:TPU:0, one launch (start us, length us, event | category | flops | bytes accessed | tf_op | source)
XLA Modules:
  0.0 87.5 jit_solution(383116428437697514)
XLA Ops:
  0.6 0.0 copy-start.9
  0.6 0.0 copy-start.11
  0.6 5.7 %shard_map.149 = bf16[32,16,256]{2,1,0:T(8,128)(2,1)} custom-call(bf16[1,64,8,48,128]{4,3,2,1,0:T(8,128)(2,1)} %field.1, f32[128,256]{1,0:T(8,128)} %constant.18.clone.base_far.base, bf16[256,768]{1,0:T(8,128)(2,1)} %constant.19.clone.ytab_far.ytab), custom_call_target="tpu_custom_call" | custom-call | flops 1610612736 | bytes 6291456 | tf_op jit(solution)/shard_map/pallas_call | solution.py:642
  6.4 7.3 %all-to-all-start = ((bf16[32,16,256]{2,1,0:T(8,128)(2,1)}), bf16[32,16,256]{2,1,0:T(8,128)(2,1)S(1)}, u32[]{:S(2)}, u32[]{:S(2)}) async-start(bf16[32,16,256]{2,1,0:T(8,128)(2,1)} %shard_map.149), calls=%async_computation | async-start | bytes 524288 | tf_op jit(solution)/shard_map/all_to_all | solution.py:614
  13.7 0.0 copy-done.9
  13.7 0.0 copy-done.11
  13.7 0.0 copy-start
  13.7 0.0 copy-start.7
  13.7 0.0 copy-start.8
  13.8 0.0 copy-start.1
  13.8 0.0 copy-start.2
  13.8 0.0 copy-start.3
  13.8 0.0 copy-start.4
  13.8 0.0 copy-start.10
  13.8 8.3 %shard_map.150.local = bf16[64,8,48,128]{3,2,1,0:T(8,128)(2,1)} custom-call(bf16[64,8,48,128]{3,2,1,0:T(8,128)(2,1)} %bitcast.1, bf16[64,64]{1,0:T(8,128)(2,1)S(1)} %copy-done.9, f32[64]{0:T(128)S(1)} %copy-done.11), custom_call_target="tpu_custom_call" | custom-call | flops 3221225472 | bytes 12582912 | tf_op jit(solution)/shard_map/pallas_call | solution.py:628
  22.1 2.2 %all-to-all-done.arrived = bf16[32,16,256]{2,1,0:T(8,128)(2,1)S(1)} async-done(((bf16[32,16,256]{2,1,0:T(8,128)(2,1)}), bf16[32,16,256]{2,1,0:T(8,128)(2,1)S(1)}, u32[]{:S(2)}, u32[]{:S(2)}) %all-to-all-start) | async-done | bytes 262176 | tf_op jit(solution)/shard_map/all_to_all | solution.py:614
  24.3 0.0 copy-done
  24.4 1.0 %shard_map.151 = (bf16[256,256]{1,0:T(8,128)(2,1)S(1)}, bf16[32,16,256]{2,1,0:T(8,128)(2,1)S(1)}) custom-call(bf16[32,16,256]{2,1,0:T(8,128)(2,1)S(1)} %all-to-all-done.arrived, bf16[64,64,128]{2,1,0:T(8,128)(2,1)S(1)} %copy-done, bf16[256,512]{1,0:T(8,128)(2,1)S(1)} %copy-done.8, bf16[512,256]{1,0:T(8,128)(2,1)S(1)} %copy-done.7), custom_call_target="tpu_custom_call" | custom-call | flops 100000000 | bytes 1048576 | tf_op jit(solution)/shard_map/pallas_call | solution.py:663
  25.4 14.0 %all_to_all.20.arrived = bf16[32,16,256]{2,1,0:T(8,128)(2,1)S(1)} all-to-all(bf16[32,16,256]{2,1,0:T(8,128)(2,1)S(1)} %get-tuple-element.13), channel_id=1, replica_groups=mesh['dp'=8,'space'=4] {'space','dp'}, dimensions={0} | all-to-all | bytes 524288 | tf_op jit(solution)/shard_map/all_to_all | solution.py:614
  39.4 0.0 copy-done.2
  39.5 13.1 %shard_map.152 = (bf16[64,8,48,128]{3,2,1,0:T(8,128)(2,1)}, bf16[32,16,256]{2,1,0:T(8,128)(2,1)}) custom-call(bf16[32,16,256]{2,1,0:T(8,128)(2,1)S(1)} %all_to_all.20.arrived, bf16[64,8,48,128]{3,2,1,0:T(8,128)(2,1)} %shard_map.150.local, bf16[1,64,8,48,128]{4,3,2,1,0:T(8,128)(2,1)} %cotangent.1, f32[128,256]{1,0:T(8,128)S(1)} %copy-done.4, ...), custom_call_target="tpu_custom_call" | custom-call | flops 3221225472 | bytes 18874368 | tf_op jit(solution)/shard_map/pallas_call | solution.py:671
  52.5 2.6 %all-to-all-start.2 = ((bf16[32,16,256]{2,1,0:T(8,128)(2,1)}), bf16[32,16,256]{2,1,0:T(8,128)(2,1)S(1)}, u32[]{:S(2)}, u32[]{:S(2)}) async-start(bf16[32,16,256]{2,1,0:T(8,128)(2,1)} %get-tuple-element.15), calls=%async_computation.2 | async-start | bytes 524288 | tf_op jit(solution)/shard_map/all_to_all | solution.py:614
  55.1 0.0 copy-start.5
  55.2 0.0 copy-start.6
  55.2 8.3 %shard_map.153.local = bf16[64,8,48,128]{3,2,1,0:T(8,128)(2,1)} custom-call(bf16[64,8,48,128]{3,2,1,0:T(8,128)(2,1)} %get-tuple-element.16.a, bf16[64,64]{1,0:T(8,128)(2,1)S(1)} %copy-done.9), custom_call_target="tpu_custom_call" | custom-call | flops 3221225472 | bytes 12582912 | tf_op jit(solution)/shard_map/pallas_call | solution.py:628
  63.4 2.4 %all-to-all-done.2.arrived = bf16[32,16,256]{2,1,0:T(8,128)(2,1)S(1)} async-done(((bf16[32,16,256]{2,1,0:T(8,128)(2,1)}), bf16[32,16,256]{2,1,0:T(8,128)(2,1)S(1)}, u32[]{:S(2)}, u32[]{:S(2)}) %all-to-all-start.2) | async-done | bytes 262176 | tf_op jit(solution)/shard_map/all_to_all | solution.py:614
  65.8 0.0 copy-done.5
  65.8 1.9 %shard_map.154 = (bf16[256,512]{1,0:T(8,128)(2,1)S(1)}, bf16[32,16,256]{2,1,0:T(8,128)(2,1)}) custom-call(bf16[32,16,256]{2,1,0:T(8,128)(2,1)S(1)} %all-to-all-done.2.arrived, bf16[64,64,128]{2,1,0:T(8,128)(2,1)S(1)} %copy-done, bf16[256,512]{1,0:T(8,128)(2,1)S(1)} %copy-done.6, bf16[512,256]{1,0:T(8,128)(2,1)S(1)} %copy-done.5), custom_call_target="tpu_custom_call" | custom-call | flops 100000000 | bytes 1048576 | tf_op jit(solution)/shard_map/pallas_call | solution.py:687
  67.7 3.5 %all-to-all-start.3 = ((bf16[32,16,256]{2,1,0:T(8,128)(2,1)}), bf16[32,16,256]{2,1,0:T(8,128)(2,1)S(1)}, u32[]{:S(2)}, u32[]{:S(2)}) async-start(bf16[32,16,256]{2,1,0:T(8,128)(2,1)} %get-tuple-element.18), calls=%async_computation.3 | async-start | bytes 524288 | tf_op jit(solution)/shard_map/all_to_all | solution.py:614
  71.2 2.1 %shard_map.156 = f32[64,64,128]{2,1,0:T(8,128)} custom-call(bf16[256,256]{1,0:T(8,128)(2,1)S(1)} %get-tuple-element.20.spec_in, bf16[256,512]{1,0:T(8,128)(2,1)S(1)} %get-tuple-element.21.pairs), custom_call_target="tpu_custom_call" | custom-call | flops 100000000 | bytes 2097152 | tf_op jit(solution)/shard_map/pallas_call | solution.py:695
  73.3 8.6 %all-to-all-done.3.arrived = bf16[32,16,256]{2,1,0:T(8,128)(2,1)S(1)} async-done(((bf16[32,16,256]{2,1,0:T(8,128)(2,1)}), bf16[32,16,256]{2,1,0:T(8,128)(2,1)S(1)}, u32[]{:S(2)}, u32[]{:S(2)}) %all-to-all-start.3) | async-done | bytes 262176 | tf_op jit(solution)/shard_map/all_to_all | solution.py:614
  81.8 5.7 %shard_map.155 = bf16[1,64,8,48,128]{4,3,2,1,0:T(8,128)(2,1)} custom-call(bf16[32,16,256]{2,1,0:T(8,128)(2,1)S(1)} %all-to-all-done.3.arrived, bf16[64,8,48,128]{3,2,1,0:T(8,128)(2,1)} %shard_map.153.local, f32[256,128]{1,0:T(8,128)S(1)} %copy-done.3, bf16[768,256]{1,0:T(8,128)(2,1)S(1)} %copy-done.1), custom_call_target="tpu_custom_call" | custom-call | flops 1610612736 | bytes 12582912 | tf_op jit(solution)/shard_map/pallas_call | solution.py:701
  (7 shorter events, 0.0 us)
Async XLA Ops:
  0.6 13.1 %copy-start.9 = (bf16[64,64]{1,0:T(8,128)(2,1)S(1)}, bf16[64,64]{1,0:T(8,128)(2,1)}, u32[]{:S(2)}) copy-start(bf16[64,64]{1,0:T(8,128)(2,1)} %b.1) | copy-start | bytes 24580
  0.6 13.1 %copy-start.11 = (f32[64]{0:T(128)S(1)}, f32[64]{0:T(128)}, u32[]{:S(2)}) copy-start(f32[64]{0:T(128)} %offsets.1) | copy-start | bytes 772
  6.4 18.0 %all-to-all-start = ((bf16[32,16,256]{2,1,0:T(8,128)(2,1)}), bf16[32,16,256]{2,1,0:T(8,128)(2,1)S(1)}, u32[]{:S(2)}, u32[]{:S(2)}) async-start(bf16[32,16,256]{2,1,0:T(8,128)(2,1)} %shard_map.149), calls=%async_computation | async-start | bytes 524288 | tf_op jit(solution)/shard_map/all_to_all | solution.py:614
  13.7 10.6 %copy-start = (bf16[64,64,128]{2,1,0:T(8,128)(2,1)S(1)}, bf16[64,64,128]{2,1,0:T(8,128)(2,1)}, u32[]{:S(2)}) copy-start(bf16[64,64,128]{2,1,0:T(8,128)(2,1)} %weights.3) | copy-start | bytes 3145732
  13.7 10.6 %copy-start.7 = (bf16[512,256]{1,0:T(8,128)(2,1)S(1)}, bf16[512,256]{1,0:T(8,128)(2,1)}, u32[]{:S(2)}) copy-start(bf16[512,256]{1,0:T(8,128)(2,1)} %constant.21.clone.line_back) | copy-start | bytes 786436
  13.7 10.6 %copy-start.8 = (bf16[256,512]{1,0:T(8,128)(2,1)S(1)}, bf16[256,512]{1,0:T(8,128)(2,1)}, u32[]{:S(2)}) copy-start(bf16[256,512]{1,0:T(8,128)(2,1)} %constant.20.clone.line) | copy-start | bytes 786436
  13.8 25.7 %copy-start.1 = (bf16[768,256]{1,0:T(8,128)(2,1)S(1)}, bf16[768,256]{1,0:T(8,128)(2,1)}, u32[]{:S(2)}) copy-start(bf16[768,256]{1,0:T(8,128)(2,1)} %constant.23.clone.ytab_back) | copy-start | bytes 1179652
  13.8 25.7 %copy-start.2 = (bf16[256,768]{1,0:T(8,128)(2,1)S(1)}, bf16[256,768]{1,0:T(8,128)(2,1)}, u32[]{:S(2)}) copy-start(bf16[256,768]{1,0:T(8,128)(2,1)} %constant.19.clone.ytab_far.ytab) | copy-start | bytes 1179652
  13.8 25.7 %copy-start.3 = (f32[256,128]{1,0:T(8,128)S(1)}, f32[256,128]{1,0:T(8,128)}, u32[]{:S(2)}) copy-start(f32[256,128]{1,0:T(8,128)} %constant.22.clone.base_back) | copy-start | bytes 393220
  13.8 25.6 %copy-start.4 = (f32[128,256]{1,0:T(8,128)S(1)}, f32[128,256]{1,0:T(8,128)}, u32[]{:S(2)}) copy-start(f32[128,256]{1,0:T(8,128)} %constant.18.clone.base_far.base) | copy-start | bytes 393220
  13.8 25.6 %copy-start.10 = (f32[1,512]{1,0:T(1,128)S(1)}, f32[1,512]{1,0:T(1,128)}, u32[]{:S(2)}) copy-start(f32[1,512]{1,0:T(1,128)} %constant.24.clone.scale) | copy-start | bytes 6148
  52.5 13.3 %all-to-all-start.2 = ((bf16[32,16,256]{2,1,0:T(8,128)(2,1)}), bf16[32,16,256]{2,1,0:T(8,128)(2,1)S(1)}, u32[]{:S(2)}, u32[]{:S(2)}) async-start(bf16[32,16,256]{2,1,0:T(8,128)(2,1)} %get-tuple-element.15), calls=%async_computation.2 | async-start | bytes 524288 | tf_op jit(solution)/shard_map/all_to_all | solution.py:614
  55.1 10.6 %copy-start.5 = (bf16[512,256]{1,0:T(8,128)(2,1)S(1)}, bf16[512,256]{1,0:T(8,128)(2,1)}, u32[]{:S(2)}) copy-start(bf16[512,256]{1,0:T(8,128)(2,1)} %constant.26.clone.line_back) | copy-start | bytes 786436
  55.2 10.6 %copy-start.6 = (bf16[256,512]{1,0:T(8,128)(2,1)S(1)}, bf16[256,512]{1,0:T(8,128)(2,1)}, u32[]{:S(2)}) copy-start(bf16[256,512]{1,0:T(8,128)(2,1)} %constant.25.clone.line) | copy-start | bytes 786436
  67.7 14.1 %all-to-all-start.3 = ((bf16[32,16,256]{2,1,0:T(8,128)(2,1)}), bf16[32,16,256]{2,1,0:T(8,128)(2,1)S(1)}, u32[]{:S(2)}, u32[]{:S(2)}) async-start(bf16[32,16,256]{2,1,0:T(8,128)(2,1)} %get-tuple-element.18), calls=%async_computation.3 | async-start | bytes 524288 | tf_op jit(solution)/shard_map/all_to_all | solution.py:614
where the time goes:
time: 88 us; the launch traced here: 87.5 us
  Pallas kernels  46 us (52%)
  blocking collectives  14 us (16%)
  starting transfers between devices  13.4 us (15%)
  waiting for transfers between devices  13.2 us (15%)
    pallas_call x2, Pallas kernels, mix_points(): pl.pallas_call(run, grid=(width // step,), in_specs=specs, out_specs=bloc...  16.5 us
    all_to_all x1, blocking collectives, exchange(): lax.all_to_all(array, mesh_axes, split_axis=0, concat_axis=0, tiled=True)  14 us
    all_to_all x3, starting transfers between devices, exchange(): lax.all_to_all(array, mesh_axes, split_axis=0, concat_axis=0, tiled=True)  13.4 us
    all_to_all x3, waiting for transfers between devices, exchange(): lax.all_to_all(array, mesh_axes, split_axis=0, concat_axis=0, tiled=True)  13.2 us
    pallas_call x1, Pallas kernels, body(): pl.pallas_call(functools.partial(slope_kernel, per, channels), in_specs=[...  13.1 us
    pallas_call x1, Pallas kernels, body(): pl.pallas_call(functools.partial(plane_kernel, per, channels), in_specs=[...  5.73 us
    pallas_call x1, Pallas kernels, body(): pl.pallas_call(functools.partial(field_kernel, per, channels), in_specs=[...  5.69 us
    pallas_call x1, Pallas kernels, body(): pl.pallas_call(functools.partial(weight_kernel, per, samples), out_shape=...  2.07 us
  transfers between devices with their start and end apart: 3, of which 3 were waited for; matrix products, arithmetic and copies ran while one was open for 0% of the time, Pallas kernels for 21%

commit v1 on v0

--- a/solution.py
+++ b/solution.py
@@ -204,7 +204,7 @@
 
     def lay(turn):
         turn = turn.reshape(2, 2, MX, slabs, length // slabs)
-        table = np.einsum("arqsx,bd->qabsdxr", turn, same)
+        table = np.einsum("arqsx,bd->qabdsxr", turn, same)
         return rounded(table.reshape(rows, samples * length * 2))
 
     return lay(forward), lay(inverse)
@@ -262,7 +262,12 @@
     table[...] = jnp.where(same, 1.0, 0.0).astype(BF16)
 
 
-def deliver(spectra, ytab, order, scale, message, per, channels):
+def turned_index(index, slabs, devices):
+    samples = devices // slabs
+    return index % samples * slabs + index // samples
+
+
+def deliver(spectra, ytab, order, scale, message, per, channels, slabs):
     groups = channels // GROUP
     rows = spectra.shape[0] // groups
     wide = spectra.shape[1] // 2
@@ -280,14 +285,17 @@
     for part in range(parts):
         block = ordered[:, part * lanes : (part + 1) * lanes]
         for j in range(MY):
-            message[j * parts + part] = block[j * count : (j + 1) * count]
-
-
-def receive(message, order_back, ytab_back, scale, held, per):
+            message[turned_index(j * parts + part, slabs, message.shape[0])] = block[j * count : (j + 1) * count]
+
+
+def receive(message, order_back, ytab_back, scale, held, per, slabs):
     parts = MZ // per
-    blocks = message[...]
-    blocks = blocks.reshape(MY, parts, *blocks.shape[1:])
-    lanes = [blocks[:, part].reshape(-1, blocks.shape[3]) for part in range(parts)]
+    lanes = [
+        jnp.concatenate(
+            [message[turned_index(j * parts + part, slabs, message.shape[0])] for j in range(MY)], axis=0
+        )
+        for part in range(parts)
+    ]
     ordered = dot(jnp.concatenate(lanes, axis=1), order_back[...]).astype(BF16)
     lines = dot(ytab_back[...], ordered)
     if scale is not None:
@@ -329,7 +337,9 @@
     groups = field.shape[0] // GROUP
     rows_z = field.shape[-1]
     rows = spectra.shape[0] // groups
-    table = ztab[pl.ds(pl.multiple_of(first * rows_z, count * rows_z), count * rows_z)]
+    start = first * rows_z
+    start = start if isinstance(first, int) else pl.multiple_of(start, count * rows_z)
+    table = ztab[pl.ds(start, count * rows_z)]
     lanes = [
         jnp.concatenate([field[g * GROUP + first + slot].reshape(rows, rows_z) for g in range(groups)], axis=0)
         for slot in range(count)
@@ -338,7 +348,7 @@
 
 
 def plane_kernel(
-    per, channels, field, base_far, ytab_far, message, ztab, order, spectra, buffer, base, ytab, sems, table_sems
+    per, channels, slabs, field, base_far, ytab_far, message, ztab, order, spectra, buffer, base, ytab, sems, table_sems
 ):
     incoming = Move(field.at[0], buffer, sems)
     base_copy = pltpu.make_async_copy(base_far, base, table_sems.at[0])
@@ -360,12 +370,12 @@
         add_spectra(buffer, ztab, step * SLOTS, SLOTS, spectra)
 
     ytab_copy.wait()
-    deliver(spectra, ytab, order, None, message, per, channels)
+    deliver(spectra, ytab, order, None, message, per, channels, slabs)
 
 
 def slope_kernel(
-    per, channels, arrived, local, cotangent, base, base_back, ytab, ytab_back, scale,
-    slope, message, ztab, ztab_back, order, held, spectra, local_in, cotangent_in, result, first_sum, second_sum,
+    per, channels, slabs, arrived, local, cotangent, base, base_back, ytab, ytab_back, scale,
+    slope, message, ztab, ztab_back, order, held, spectra, local_in, cotangent_in, result, sums_a, sums_b, sums_c, sums_d,
     local_sems, cotangent_sems, result_sems,
 ):
     width, rows_y, rows_z = local.shape[1:]
@@ -376,7 +386,7 @@
     outgoing = Move(result, slope, result_sems)
     start_all(incoming, 0)
     fill_order(per, channels, True, order)
-    receive(arrived, order, ytab_back, scale, held, per)
+    receive(arrived, order, ytab_back, scale, held, per, slabs)
     start_all(incoming, 1)
     fill_z_back(base_back, ztab_back)
     fill_z(base, ztab)
@@ -385,13 +395,19 @@
     spectra[...] = jnp.zeros_like(spectra)
     start_all(incoming, 3)
 
-    @pl.loop(0, STEPS)
-    def _(step):
+    totals = ((sums_a, sums_b), (sums_c, sums_d))
+
+    def synthesise(step):
+        for pair, total in enumerate(totals[step % 2]):
+            total[...] = dot(held[...], ztab_back[step, :, 2 * pair * rows_z : 2 * (pair + 1) * rows_z])
+
+    synthesise(0)
+    for step in range(STEPS):
         for each in incoming:
             each.wait(step)
-        for pair, total in enumerate((first_sum, second_sum)):
-            total[...] = dot(held[...], ztab_back[step, :, 2 * pair * rows_z : 2 * (pair + 1) * rows_z])
-        for pair, total in enumerate((first_sum, second_sum)):
+        if step + 1 < STEPS:
+            synthesise(step + 1)
+        for pair, total in enumerate(totals[step % 2]):
             for g in range(groups):
                 for offset in range(2):
                     c = g * GROUP + step * SLOTS + 2 * pair + offset
@@ -405,13 +421,13 @@
             add_spectra(result, ztab, step * SLOTS + 2 * pair, 2, spectra)
         outgoing.start(step)
 
-    deliver(spectra, ytab, order, scale, message, per, channels)
+    deliver(spectra, ytab, order, scale, message, per, channels, slabs)
     for step in range(STEPS):
         outgoing.wait(step)
 
 
 def field_kernel(
-    per, channels, arrived, local, base_back, ytab_back, out, ztab_back, order, held, local_in, result,
+    per, channels, slabs, arrived, local, base_back, ytab_back, out, ztab_back, order, held, local_in, result,
     local_sems, result_sems,
 ):
     width, rows_y, rows_z = local.shape[1:]
@@ -422,7 +438,7 @@
     incoming.start(0)
     fill_order(per, channels, True, order)
     incoming.start(1)
-    receive(arrived, order, ytab_back, None, held, per)
+    receive(arrived, order, ytab_back, None, held, per, slabs)
     incoming.start(2)
     fill_z_back(base_back, ztab_back)
     incoming.start(3)
@@ -640,7 +656,7 @@
         )(*operands)
 
     planes = pl.pallas_call(
-        functools.partial(plane_kernel, per, channels),
+        functools.partial(plane_kernel, per, channels, slabs),
         in_specs=[far, far, far],
         out_specs=whole(message),
         out_shape=message,
@@ -669,16 +685,16 @@
     )(arrived, mode_weights, line_fwd, inv_t)
     returned = exchange(mixed)
     slope, back_plane = pl.pallas_call(
-        functools.partial(slope_kernel, per, channels),
+        functools.partial(slope_kernel, per, channels, slabs),
         in_specs=[whole(message), far, far]
         + [whole(t) for t in (base, base_t, ytab, ytab_t, scale)],
         out_specs=(far, whole(message)),
         out_shape=(far_field, message),
         scratch_shapes=[ztab, ztab_t, order, held, sums]
         + [buffer] * 3
-        + [pair_sums] * 2
+        + [pair_sums] * 4
         + [sems] * 3,
-        compiler_params=params(32),
+        compiler_params=params(40),
         cost_estimate=cost(2 * plane_flops, 6 * count, 2 * count),
     )(returned, kept_far(local), kept_far(cotangent), base, base_t, ytab, ytab_t, scale)
     arrived_back = exchange(back_plane)
@@ -699,7 +715,7 @@
         cost_estimate=cost(10**8, 4 * mode_weights.size),
     )(spec_in, pairs)
     grad_in = pl.pallas_call(
-        functools.partial(field_kernel, per, channels),
+        functools.partial(field_kernel, per, channels, slabs),
         in_specs=[whole(message), far, whole(base_t), whole(ytab_t)],
         out_specs=far,
         out_shape=shaped(activations.shape, BF16),
@@ -730,7 +746,7 @@
     slabs = mesh.shape["space"]
     devices = slabs * mesh.shape["dp"]
     return jax.shard_map(
-        functools.partial(chosen_body, ("space", "dp"), devices, slabs),
+        functools.partial(chosen_body, ("dp", "space"), devices, slabs),
         mesh=mesh,
         in_specs=(
             P("dp", None, "space", None, None),

time: 88 us -> 88.7 us (level)
  no operation moved by 1% of the time
where the time goes in v1:
time: 88.7 us; the launch traced here: 88.3 us
  Pallas kernels  46.7 us (53%)
  blocking collectives  14.1 us (16%)
  starting transfers between devices  13.4 us (15%)
  waiting for transfers between devices  13 us (15%)
  between operations  0.98 us (1%)
    pallas_call x2, Pallas kernels, mix_points(): pl.pallas_call(run, grid=(width // step,), in_specs=specs, out_specs=bloc...  16.5 us
    all_to_all x1, blocking collectives, exchange(): lax.all_to_all(array, mesh_axes, split_axis=0, concat_axis=0, tiled=True)  14.1 us
    pallas_call x1, Pallas kernels, body(): pl.pallas_call(functools.partial(slope_kernel, per, channels, slabs), in_...  13.7 us
    all_to_all x3, starting transfers between devices, exchange(): lax.all_to_all(array, mesh_axes, split_axis=0, concat_axis=0, tiled=True)  13.4 us
    all_to_all x3, waiting for transfers between devices, exchange(): lax.all_to_all(array, mesh_axes, split_axis=0, concat_axis=0, tiled=True)  13 us
    pallas_call x1, Pallas kernels, body(): pl.pallas_call(functools.partial(plane_kernel, per, channels, slabs), in_...  5.74 us
    pallas_call x1, Pallas kernels, body(): pl.pallas_call(functools.partial(field_kernel, per, channels, slabs), in_...  5.69 us
    pallas_call x1, Pallas kernels, body(): pl.pallas_call(functools.partial(weight_kernel, per, samples), out_shape=...  2.07 us
  transfers between devices with their start and end apart: 3, of which 3 were waited for; matrix products, arithmetic and copies ran while one was open for 0% of the time, Pallas kernels for 21%

profile of v1, /device:TPU:0, one launch (start us, length us, event | category | flops | bytes accessed | tf_op | source)
XLA Modules:
  0.0 88.3 jit_solution(16854212463269597399)
XLA Ops:
  0.6 0.0 copy-start.9
  0.6 0.0 copy-start.11
  0.6 5.7 %shard_map.149 = bf16[32,16,256]{2,1,0:T(8,128)(2,1)} custom-call(bf16[1,64,8,48,128]{4,3,2,1,0:T(8,128)(2,1)} %field.1, f32[128,256]{1,0:T(8,128)} %constant.18.clone.base_far.base, bf16[256,768]{1,0:T(8,128)(2,1)} %constant.19.clone.ytab_far.ytab), custom_call_target="tpu_custom_call" | custom-call | flops 1610612736 | bytes 6291456 | tf_op jit(solution)/shard_map/pallas_call | solution.py:658
  6.4 7.3 %all-to-all-start = ((bf16[32,16,256]{2,1,0:T(8,128)(2,1)}), bf16[32,16,256]{2,1,0:T(8,128)(2,1)S(1)}, u32[]{:S(2)}, u32[]{:S(2)}) async-start(bf16[32,16,256]{2,1,0:T(8,128)(2,1)} %shard_map.149), calls=%async_computation | async-start | bytes 524288 | tf_op jit(solution)/shard_map/all_to_all | solution.py:630
  13.7 0.0 copy-done.9
  13.7 0.0 copy-done.11
  13.7 0.0 copy-start
  13.7 0.0 copy-start.7
  13.7 0.0 copy-start.8
  13.8 0.0 copy-start.1
  13.8 0.0 copy-start.2
  13.8 0.0 copy-start.3
  13.8 0.0 copy-start.4
  13.8 0.0 copy-start.10
  13.8 8.3 %shard_map.150.local = bf16[64,8,48,128]{3,2,1,0:T(8,128)(2,1)} custom-call(bf16[64,8,48,128]{3,2,1,0:T(8,128)(2,1)} %bitcast.1, bf16[64,64]{1,0:T(8,128)(2,1)S(1)} %copy-done.9, f32[64]{0:T(128)S(1)} %copy-done.11), custom_call_target="tpu_custom_call" | custom-call | flops 3221225472 | bytes 12582912 | tf_op jit(solution)/shard_map/pallas_call | solution.py:644
  22.1 2.2 %all-to-all-done.arrived = bf16[32,16,256]{2,1,0:T(8,128)(2,1)S(1)} async-done(((bf16[32,16,256]{2,1,0:T(8,128)(2,1)}), bf16[32,16,256]{2,1,0:T(8,128)(2,1)S(1)}, u32[]{:S(2)}, u32[]{:S(2)}) %all-to-all-start) | async-done | bytes 262176 | tf_op jit(solution)/shard_map/all_to_all | solution.py:630
  24.3 1.0 %shard_map.151 = (bf16[256,256]{1,0:T(8,128)(2,1)S(1)}, bf16[32,16,256]{2,1,0:T(8,128)(2,1)S(1)}) custom-call(bf16[32,16,256]{2,1,0:T(8,128)(2,1)S(1)} %all-to-all-done.arrived, bf16[64,64,128]{2,1,0:T(8,128)(2,1)S(1)} %copy-done, bf16[256,512]{1,0:T(8,128)(2,1)S(1)} %copy-done.8, bf16[512,256]{1,0:T(8,128)(2,1)S(1)} %copy-done.7), custom_call_target="tpu_custom_call" | custom-call | flops 100000000 | bytes 1048576 | tf_op jit(solution)/shard_map/pallas_call | solution.py:679
  25.3 14.1 %all_to_all.20.arrived = bf16[32,16,256]{2,1,0:T(8,128)(2,1)S(1)} all-to-all(bf16[32,16,256]{2,1,0:T(8,128)(2,1)S(1)} %get-tuple-element.13), channel_id=1, replica_groups=mesh['dp'=8,'space'=4] {'dp','space'}, dimensions={0} | all-to-all | bytes 524288 | tf_op jit(solution)/shard_map/all_to_all | solution.py:630
  39.4 0.0 copy-done.4
  39.4 0.0 copy-done.10
  39.4 13.7 %shard_map.152 = (bf16[64,8,48,128]{3,2,1,0:T(8,128)(2,1)}, bf16[32,16,256]{2,1,0:T(8,128)(2,1)}) custom-call(bf16[32,16,256]{2,1,0:T(8,128)(2,1)S(1)} %all_to_all.20.arrived, bf16[64,8,48,128]{3,2,1,0:T(8,128)(2,1)} %shard_map.150.local, bf16[1,64,8,48,128]{4,3,2,1,0:T(8,128)(2,1)} %cotangent.1, f32[128,256]{1,0:T(8,128)S(1)} %copy-done.4, ...), custom_call_target="tpu_custom_call" | custom-call | flops 3221225472 | bytes 18874368 | tf_op jit(solution)/shard_map/pallas_call | solution.py:687
  53.2 2.6 %all-to-all-start.2 = ((bf16[32,16,256]{2,1,0:T(8,128)(2,1)}), bf16[32,16,256]{2,1,0:T(8,128)(2,1)S(1)}, u32[]{:S(2)}, u32[]{:S(2)}) async-start(bf16[32,16,256]{2,1,0:T(8,128)(2,1)} %get-tuple-element.15), calls=%async_computation.2 | async-start | bytes 524288 | tf_op jit(solution)/shard_map/all_to_all | solution.py:630
  55.8 0.0 copy-start.5
  55.8 0.0 copy-start.6
  55.8 8.3 %shard_map.153.local = bf16[64,8,48,128]{3,2,1,0:T(8,128)(2,1)} custom-call(bf16[64,8,48,128]{3,2,1,0:T(8,128)(2,1)} %get-tuple-element.16.a, bf16[64,64]{1,0:T(8,128)(2,1)S(1)} %copy-done.9), custom_call_target="tpu_custom_call" | custom-call | flops 3221225472 | bytes 12582912 | tf_op jit(solution)/shard_map/pallas_call | solution.py:644
  64.1 2.3 %all-to-all-done.2.arrived = bf16[32,16,256]{2,1,0:T(8,128)(2,1)S(1)} async-done(((bf16[32,16,256]{2,1,0:T(8,128)(2,1)}), bf16[32,16,256]{2,1,0:T(8,128)(2,1)S(1)}, u32[]{:S(2)}, u32[]{:S(2)}) %all-to-all-start.2) | async-done | bytes 262176 | tf_op jit(solution)/shard_map/all_to_all | solution.py:630
  66.4 0.0 copy-done.6
  66.4 1.9 %shard_map.154 = (bf16[256,512]{1,0:T(8,128)(2,1)S(1)}, bf16[32,16,256]{2,1,0:T(8,128)(2,1)}) custom-call(bf16[32,16,256]{2,1,0:T(8,128)(2,1)S(1)} %all-to-all-done.2.arrived, bf16[64,64,128]{2,1,0:T(8,128)(2,1)S(1)} %copy-done, bf16[256,512]{1,0:T(8,128)(2,1)S(1)} %copy-done.6, bf16[512,256]{1,0:T(8,128)(2,1)S(1)} %copy-done.5), custom_call_target="tpu_custom_call" | custom-call | flops 100000000 | bytes 1048576 | tf_op jit(solution)/shard_map/pallas_call | solution.py:703
  68.3 3.5 %all-to-all-start.3 = ((bf16[32,16,256]{2,1,0:T(8,128)(2,1)}), bf16[32,16,256]{2,1,0:T(8,128)(2,1)S(1)}, u32[]{:S(2)}, u32[]{:S(2)}) async-start(bf16[32,16,256]{2,1,0:T(8,128)(2,1)} %get-tuple-element.18), calls=%async_computation.3 | async-start | bytes 524288 | tf_op jit(solution)/shard_map/all_to_all | solution.py:630
  71.8 2.1 %shard_map.156 = f32[64,64,128]{2,1,0:T(8,128)} custom-call(bf16[256,256]{1,0:T(8,128)(2,1)S(1)} %get-tuple-element.20.spec_in, bf16[256,512]{1,0:T(8,128)(2,1)S(1)} %get-tuple-element.21.pairs), custom_call_target="tpu_custom_call" | custom-call | flops 100000000 | bytes 2097152 | tf_op jit(solution)/shard_map/pallas_call | solution.py:711
  73.9 8.5 %all-to-all-done.3.arrived = bf16[32,16,256]{2,1,0:T(8,128)(2,1)S(1)} async-done(((bf16[32,16,256]{2,1,0:T(8,128)(2,1)}), bf16[32,16,256]{2,1,0:T(8,128)(2,1)S(1)}, u32[]{:S(2)}, u32[]{:S(2)}) %all-to-all-start.3) | async-done | bytes 262176 | tf_op jit(solution)/shard_map/all_to_all | solution.py:630
  82.4 5.7 %shard_map.155 = bf16[1,64,8,48,128]{4,3,2,1,0:T(8,128)(2,1)} custom-call(bf16[32,16,256]{2,1,0:T(8,128)(2,1)S(1)} %all-to-all-done.3.arrived, bf16[64,8,48,128]{3,2,1,0:T(8,128)(2,1)} %shard_map.153.local, f32[256,128]{1,0:T(8,128)S(1)} %copy-done.3, bf16[768,256]{1,0:T(8,128)(2,1)S(1)} %copy-done.1), custom_call_target="tpu_custom_call" | custom-call | flops 1610612736 | bytes 12582912 | tf_op jit(solution)/shard_map/pallas_call | solution.py:717
  (7 shorter events, 0.0 us)
Async XLA Ops:
  0.6 13.1 %copy-start.9 = (bf16[64,64]{1,0:T(8,128)(2,1)S(1)}, bf16[64,64]{1,0:T(8,128)(2,1)}, u32[]{:S(2)}) copy-start(bf16[64,64]{1,0:T(8,128)(2,1)} %b.1) | copy-start | bytes 24580
  0.6 13.1 %copy-start.11 = (f32[64]{0:T(128)S(1)}, f32[64]{0:T(128)}, u32[]{:S(2)}) copy-start(f32[64]{0:T(128)} %offsets.1) | copy-start | bytes 772
  6.4 17.9 %all-to-all-start = ((bf16[32,16,256]{2,1,0:T(8,128)(2,1)}), bf16[32,16,256]{2,1,0:T(8,128)(2,1)S(1)}, u32[]{:S(2)}, u32[]{:S(2)}) async-start(bf16[32,16,256]{2,1,0:T(8,128)(2,1)} %shard_map.149), calls=%async_computation | async-start | bytes 524288 | tf_op jit(solution)/shard_map/all_to_all | solution.py:630
  13.7 10.6 %copy-start = (bf16[64,64,128]{2,1,0:T(8,128)(2,1)S(1)}, bf16[64,64,128]{2,1,0:T(8,128)(2,1)}, u32[]{:S(2)}) copy-start(bf16[64,64,128]{2,1,0:T(8,128)(2,1)} %weights.3) | copy-start | bytes 3145732
  13.7 10.6 %copy-start.7 = (bf16[512,256]{1,0:T(8,128)(2,1)S(1)}, bf16[512,256]{1,0:T(8,128)(2,1)}, u32[]{:S(2)}) copy-start(bf16[512,256]{1,0:T(8,128)(2,1)} %constant.21.clone.line_back) | copy-start | bytes 786436
  13.7 10.6 %copy-start.8 = (bf16[256,512]{1,0:T(8,128)(2,1)S(1)}, bf16[256,512]{1,0:T(8,128)(2,1)}, u32[]{:S(2)}) copy-start(bf16[256,512]{1,0:T(8,128)(2,1)} %constant.20.clone.line) | copy-start | bytes 786436
  13.8 25.6 %copy-start.1 = (bf16[768,256]{1,0:T(8,128)(2,1)S(1)}, bf16[768,256]{1,0:T(8,128)(2,1)}, u32[]{:S(2)}) copy-start(bf16[768,256]{1,0:T(8,128)(2,1)} %constant.23.clone.ytab_back) | copy-start | bytes 1179652
  13.8 25.6 %copy-start.2 = (bf16[256,768]{1,0:T(8,128)(2,1)S(1)}, bf16[256,768]{1,0:T(8,128)(2,1)}, u32[]{:S(2)}) copy-start(bf16[256,768]{1,0:T(8,128)(2,1)} %constant.19.clone.ytab_far.ytab) | copy-start | bytes 1179652
  13.8 25.6 %copy-start.3 = (f32[256,128]{1,0:T(8,128)S(1)}, f32[256,128]{1,0:T(8,128)}, u32[]{:S(2)}) copy-start(f32[256,128]{1,0:T(8,128)} %constant.22.clone.base_back) | copy-start | bytes 393220
  13.8 25.6 %copy-start.4 = (f32[128,256]{1,0:T(8,128)S(1)}, f32[128,256]{1,0:T(8,128)}, u32[]{:S(2)}) copy-start(f32[128,256]{1,0:T(8,128)} %constant.18.clone.base_far.base) | copy-start | bytes 393220
  13.8 25.6 %copy-start.10 = (f32[1,512]{1,0:T(1,128)S(1)}, f32[1,512]{1,0:T(1,128)}, u32[]{:S(2)}) copy-start(f32[1,512]{1,0:T(1,128)} %constant.24.clone.scale) | copy-start | bytes 6148
  53.2 13.2 %all-to-all-start.2 = ((bf16[32,16,256]{2,1,0:T(8,128)(2,1)}), bf16[32,16,256]{2,1,0:T(8,128)(2,1)S(1)}, u32[]{:S(2)}, u32[]{:S(2)}) async-start(bf16[32,16,256]{2,1,0:T(8,128)(2,1)} %get-tuple-element.15), calls=%async_computation.2 | async-start | bytes 524288 | tf_op jit(solution)/shard_map/all_to_all | solution.py:630
  55.8 10.6 %copy-start.5 = (bf16[512,256]{1,0:T(8,128)(2,1)S(1)}, bf16[512,256]{1,0:T(8,128)(2,1)}, u32[]{:S(2)}) copy-start(bf16[512,256]{1,0:T(8,128)(2,1)} %constant.26.clone.line_back) | copy-start | bytes 786436
  55.8 10.6 %copy-start.6 = (bf16[256,512]{1,0:T(8,128)(2,1)S(1)}, bf16[256,512]{1,0:T(8,128)(2,1)}, u32[]{:S(2)}) copy-start(bf16[256,512]{1,0:T(8,128)(2,1)} %constant.25.clone.line) | copy-start | bytes 786436
  68.3 14.1 %all-to-all-start.3 = ((bf16[32,16,256]{2,1,0:T(8,128)(2,1)}), bf16[32,16,256]{2,1,0:T(8,128)(2,1)S(1)}, u32[]{:S(2)}, u32[]{:S(2)}) async-start(bf16[32,16,256]{2,1,0:T(8,128)(2,1)} %get-tuple-element.18), calls=%async_computation.3 | async-start | bytes 524288 | tf_op jit(solution)/shard_map/all_to_all | solution.py:630
